TPU v7x, 32 devices: a whole 2x2x4 slice. The times are simulated.
32 devices in a mesh: gx: 4 (over z), gy: 2 (over x), gz: 4 (over y, core).
Axes of the slice: x: 2, y: 2, z: 4, core: 2. Of those that a mesh axis runs over, the one named last changes fastest.
Arguments:
- inputs: bfloat16 [1024, 12288], P('gx', 'gz'), may hold values from -6 to 6
- weight: bfloat16 [12288, 24576], P(('gz', 'gx'), 'gy'), may hold values from -0.0546875 to 0.0546875
- grad_out: bfloat16 [1024, 24576], P(('gx', 'gz'), 'gy'), may hold values from -6 to 6
- pre_act: bfloat16 [1024, 24576], P(('gx', 'gz'), 'gy'), may hold values from -6 to 6
Outputs:
- grad_in: bfloat16 [1024, 12288], P('gx', 'gz')
- grad_weight: bfloat16 [12288, 24576], P(('gz', 'gx'), 'gy')
All inputs are finite; a program needn't handle non-finite values.
Results may differ from a plain program's by a relative error of at most 0.0049.
Values may be sent and summed in bfloat16 or wider, within the bound.
A program may use at most 128 MiB of HBM per device.

v0:
```python
import jax
import jax.numpy as jnp
from jax import lax
from jax.sharding import PartitionSpec as P


def gelu_slope(value):
    scale = 0.7978845608028654
    tangent = jnp.tanh(scale * (value + 0.044715 * value * value * value))
    inner = scale * (1.0 + 3.0 * 0.044715 * value * value)
    return 0.5 * (1.0 + tangent) + 0.5 * value * (1.0 - tangent * tangent) * inner


def shards(inputs, weight, grad_out, pre_act):
    grad_hidden = (grad_out.astype(jnp.float32) * gelu_slope(pre_act.astype(jnp.float32))).astype(
        jnp.bfloat16
    )
    input_cols = lax.all_to_all(inputs, "gx", split_axis=1, concat_axis=0, tiled=True)
    piece = lax.all_gather(grad_hidden, ("gx", "gz"), axis=0, tiled=True)
    weight_sum = lax.dot_general(
        input_cols, piece, (((0,), (0,)), ((), ())), preferred_element_type=jnp.float32
    )
    product = lax.dot_general(
        piece, weight, (((1,), (1,)), ((), ())), preferred_element_type=jnp.float32
    )
    input_part = product
    totals = (weight_sum, input_part)
    weight_sum, input_part = totals
    summed = lax.psum(input_part, "gy").astype(jnp.bfloat16)
    grad_in = lax.all_to_all(summed, "gx", split_axis=0, concat_axis=1, tiled=True)
    return (grad_in, weight_sum.astype(jnp.bfloat16))


def solution(mesh):
    in_specs = (P("gx", "gz"), P(("gz", "gx"), "gy"), P(("gx", "gz"), "gy"), P(("gx", "gz"), "gy"))
    out_specs = (P("gx", "gz"), P(("gz", "gx"), "gy"))
    return jax.shard_map(shards, mesh=mesh, in_specs=in_specs, out_specs=out_specs, check_vma=False)
```

profile of v0, /device:TPU:0, one launch (start us, length us, event | category | flops | bytes accessed | tf_op | source)
XLA Modules:
  0.0 339.3 jit_solution(7021314442229046615)
XLA Ops:
  7.2 0.0 copy-start
  7.2 0.0 all-gather.2.cloned.1.call-start
  7.2 4.6 %fusion.7 = bf16[64,12288]{1,0:T(8,128)(2,1)} fusion(bf16[64,12288]{1,0:T(8,128)(2,1)} %param.7, bf16[64,12288]{1,0:T(8,128)(2,1)} %param.6), kind=kLoop, calls=%fused_computation.15 | loop fusion | flops 16515072 | bytes 4718592 | tf_op jit(solution)/shard_map/convert_element_type | solution.py:15
  11.8 0.0 all-gather.2.cloned.1.call-update
  11.8 0.0 copy-done
  11.8 0.7 copy.11
  12.5 59.6 %all_to_all.38 = bf16[256,4,768]{0,2,1:T(8,128)(2,1)S(1)} all-to-all(bf16[256,4,768]{0,2,1:T(8,128)(2,1)S(1)} %bitcast.15), channel_id=1, replica_groups=mesh['gx'=4,'gy'=2,'gz'=4] {'gx'}, dimensions={1} | all-to-all | bytes 3145728 | tf_op jit(solution)/shard_map/all_to_all | solution.py:18
  72.2 1.6 copy.12
  73.7 92.6 %all-gather.2.cloned.1.call-done = bf16[1024,12288]{1,0:T(8,128)(2,1)} async-done(((bf16[64,12288]{1,0:T(8,128)(2,1)}), bf16[1024,12288]{1,0:T(8,128)(2,1)}) %all-gather.2.cloned.1.call-update) | async-done | bytes 25165840 | tf_op jit(solution)/shard_map/all_gather | solution.py:19
  166.3 24.7 %fusion.10 = f32[1024,768]{1,0:T(8,128)S(1)} fusion(bf16[1024,12288]{1,0:T(8,128)(2,1)} %all-gather.2.cloned.1.call-done, bf16[768,12288]{1,0:T(8,128)(2,1)} %param.5), kind=kOutput, calls=%fused_computation.18 | convolution fusion | flops 19327352832 | bytes 47185920 | tf_op jit(solution)/shard_map/dot_general | solution.py:23
  191.1 77.5 %all-reduce.1 = bf16[1024,768]{1,0:T(8,128)(2,1)} all-reduce(f32[1024,768]{1,0:T(8,128)S(1)} %fusion.10), channel_id=1, replica_groups=mesh['gx'=4,'gy'=2,'gz'=4] {'gy'}, use_global_device_ids=true, to_apply=%region_0.0 | all-reduce | flops 786432 | bytes 4718592 | tf_op jit(solution)/shard_map/psum | solution.py:29
  268.6 0.0 copy-start.1
  268.6 11.3 %all-to-all-start = ((bf16[4,256,768]{2,1,0:T(8,128)(2,1)}), bf16[4,256,768]{2,1,0:T(8,128)(2,1)S(1)}, u32[]{:S(2)}, u32[]{:S(2)}) async-start(bf16[4,256,768]{2,1,0:T(8,128)(2,1)} %bitcast), calls=%async_computation | async-start | bytes 3145728 | tf_op jit(solution)/shard_map/all_to_all | solution.py:30
  279.9 0.0 copy-done.1
  279.9 26.6 %fusion = bf16[768,12288]{0,1:T(8,128)(2,1)} fusion(bf16[1024,12288]{1,0:T(8,128)(2,1)} %all-gather.2.cloned.1.call-done, bf16[1024,768]{1,0:T(8,128)(2,1)S(1)} %bitcast.16), kind=kOutput, calls=%fused_computation.1 | convolution fusion | flops 19336790016 | bytes 45613056 | tf_op jit(solution)/shard_map/dot_general | solution.py:20
  306.6 24.6 %copy.13 = bf16[768,12288]{1,0:T(8,128)(2,1)} copy(bf16[768,12288]{0,1:T(8,128)(2,1)} %fusion) | data formatting | bytes 37748736
  331.1 0.0 all-to-all-done
  331.1 1.3 copy.14
Async XLA Ops:
  7.2 4.6 %copy-start = (bf16[256,3072]{1,0:T(8,128)(2,1)S(1)}, bf16[256,3072]{1,0:T(8,128)(2,1)}, u32[]{:S(2)}) copy-start(bf16[256,3072]{1,0:T(8,128)(2,1)} %param.4) | copy-start | bytes 4718596
  7.2 159.2 %all-gather.2.cloned.1.call-start = ((), (), s32[]{:S(2)}) async-start(), calls=%async_computation.2 | async-start | bytes 26738688 | tf_op jit(solution)/shard_map/all_gather | solution.py:19
  268.6 11.3 %copy-start.1 = (bf16[4,256,768]{2,1,0:T(8,128)(2,1)S(1)}, bf16[4,256,768]{2,1,0:T(8,128)(2,1)}, u32[]{:S(2)}) copy-start(bf16[4,256,768]{2,1,0:T(8,128)(2,1)} %copy.12) | copy-start | bytes 4718596
  268.6 62.5 %all-to-all-start = ((bf16[4,256,768]{2,1,0:T(8,128)(2,1)}), bf16[4,256,768]{2,1,0:T(8,128)(2,1)S(1)}, u32[]{:S(2)}, u32[]{:S(2)}) async-start(bf16[4,256,768]{2,1,0:T(8,128)(2,1)} %bitcast), calls=%async_computation | async-start | bytes 3145728 | tf_op jit(solution)/shard_map/all_to_all | solution.py:30
Sparse Core Ops, SparseCore 0:
  11.9 154.3 all-gather.1
where the time goes:
time: 340 us; the launch traced here: 339 us
  blocking collectives  137 us (40%)
  waiting for transfers between devices  92.6 us (27%)
  matrix products  51.4 us (15%)
  local copies, waits for them, and re-layouts  28.2 us (8%)
  between operations  14.1 us (4%)
  starting transfers between devices  11.3 us (3%)
  other arithmetic  4.56 us (1%)
    all_gather x1, waiting for transfers between devices, shards(): piece = lax.all_gather(grad_hidden, ('gx', 'gz'), axis=0, tiled=True)  92.6 us
    psum x1, blocking collectives, shards(): summed = lax.psum(input_part, 'gy').astype(jnp.bfloat16)  77.5 us
    all_to_all x1, blocking collectives, shards(): lax.all_to_all(inputs, 'gx', split_axis=1, concat_axis=0, tiled=True)  59.6 us
    dot_general x1, matrix products, shards(): lax.dot_general(input_cols, piece, (((0,), (0,)), ((), ())), preferred_el...  26.6 us
    unnamed x6, local copies, waits for them, and re-layouts  25.3 us
    dot_general x1, matrix products, shards(): lax.dot_general(piece, weight, (((1,), (1,)), ((), ())), preferred_elemen...  24.7 us
    all_to_all x1, starting transfers between devices, shards(): lax.all_to_all(summed, 'gx', split_axis=0, concat_axis=1, tiled=True)  11.3 us
  transfers between devices with their start and end apart: 2, of which 1 were waited for; matrix products, arithmetic and copies ran while one was open for 16% of the time, Pallas kernels for 0%

commit v1 on v0

v1 whole, which is shorter than its diff:
```python
import functools

import jax
import jax.numpy as jnp
from jax import lax
from jax.experimental import pallas as pl
from jax.experimental.pallas import tpu as pltpu
from jax.sharding import PartitionSpec as P

MESH = pl.DeviceIdType.MESH
F32 = jnp.float32
BF16 = jnp.bfloat16
UP, DOWN, ACROSS, TWIN = 0, 1, 2, 3


def gelu_slope(value):
    scale = 0.7978845608028654
    tangent = jnp.tanh(scale * (value + 0.044715 * value * value * value))
    inner = scale * (1.0 + 3.0 * 0.044715 * value * value)
    return 0.5 * (1.0 + tangent) + 0.5 * value * (1.0 - tangent * tangent) * inner


def kernel(
    nz, chunks,
    go, pa, x_hbm, w_hbm,
    gi_out, gw_out,
    gh, w, xs, xt, acc, psend, precv, osend, gin, stage,
    ring_send, ring_recv, x_send, x_recv, p_send, p_recv, o_send, o_recv, w_sem, gw_sem, gi_sem,
):
    z, x, q = lax.axis_index("gx"), lax.axis_index("gy"), lax.axis_index("gz")
    rows = go.shape[0]
    group = 4 * rows
    half = group // 2
    hidden = gh.shape[1]
    wide = hidden // chunks
    depth = w.shape[0]
    twin = q + 1 - 2 * lax.rem(q, 2)
    across = lax.rem(q + 2, 4)
    diagonal = lax.rem(twin + 2, 4)

    def at(zz, xx, qq):
        return (zz, xx, qq)

    barrier = pltpu.get_barrier_semaphore()
    for k in range(1, nz):
        for xx in (x, 1 - x):
            pl.semaphore_signal(
                barrier, inc=1, device_id=at(lax.rem(z + k, nz), xx, q), device_id_type=MESH
            )
    for partner in (at(z, 1 - x, q), at(z, x, twin), at(z, x, across)):
        pl.semaphore_signal(barrier, inc=1, device_id=partner, device_id_type=MESH)

    w_copy = pltpu.make_async_copy(w_hbm, w, w_sem)
    w_copy.start()

    def columns(c):
        return pl.ds(pl.multiple_of(c * wide, wide), wide)

    def block(zz, qq, cols):
        return gh.at[pl.ds(pl.multiple_of(zz * group + qq * rows, rows), rows), cols]

    def partner(kind):
        return (at(z + 1, x, q), at(z - 1, x, q), at(z, x, across), at(z, x, twin))[kind]

    def move(kind, zz, qq, cols, c):
        return pltpu.make_async_remote_copy(
            src_ref=block(zz, qq, cols),
            dst_ref=block(zz, qq, cols),
            send_sem=ring_send.at[kind, zz, qq],
            recv_sem=ring_recv.at[zz, qq, c],
            device_id=partner(kind),
            device_id_type=MESH,
        )

    def send(kind, zz, qq, c):
        move(kind, zz, qq, columns(c), c).start()

    def arrived(zz, qq, c):
        move(TWIN, zz, qq, columns(c), c).wait_recv()

    def up_or_down(kind, zz, c):
        if kind == UP:
            pl.when(z < nz - 1)(lambda: send(UP, zz, q, c))
        else:
            pl.when(z > 0)(lambda: send(DOWN, zz, q, c))

    narrow = min(256, wide)

    def make_own(c, _):
        def piece(i, _):
            cols = pl.ds(pl.multiple_of(c * wide + i * narrow, narrow), narrow)
            value = go[:, cols].astype(F32) * gelu_slope(pa[:, cols].astype(F32))
            block(z, q, cols)[...] = value.astype(BF16)
            return 0

        lax.fori_loop(0, wide // narrow, piece, 0)

        @pl.when(c == 0)
        def _():
            pl.semaphore_wait(barrier, 2 * (nz - 1) + 3)

        up_or_down(UP, z, c)
        up_or_down(DOWN, z, c)
        send(ACROSS, z, q, c)
        send(TWIN, z, q, c)
        return 0

    lax.fori_loop(0, chunks, make_own, 0)
    w_copy.wait()

    def x_move(zt, zs):
        return pltpu.make_async_remote_copy(
            src_ref=x_hbm.at[:, pl.ds(pl.multiple_of(zt * depth, depth), depth)],
            dst_ref=xs.at[pl.ds(pl.multiple_of(zs * group, group), group), :],
            send_sem=x_send.at[zt],
            recv_sem=x_recv.at[zs],
            device_id=at(zt, x, q),
            device_id_type=MESH,
        )

    own_x = pltpu.make_async_copy(
        x_hbm.at[:, pl.ds(pl.multiple_of(z * depth, depth), depth)],
        xs.at[pl.ds(pl.multiple_of(z * group, group), group), :],
        x_recv.at[z],
    )

    def sources(j):
        if j == 0:
            return [(0, z, None)]
        return [(0, z - j, z >= j), (1, z + j, z + j < nz)]

    def when(condition, body):
        if condition is None:
            body()
        else:
            pl.when(condition)(body)

    tile = min(256, depth)

    def add_input(slot, zz, c):
        tokens = pl.ds(pl.multiple_of(zz * group, group), group)

        def piece(i, _):
            out = pl.ds(pl.multiple_of(i * tile, tile), tile)
            part = lax.dot_general(
                gh[tokens, columns(c)], w[out, columns(c)],
                (((1,), (1,)), ((), ())), preferred_element_type=F32,
            )

            @pl.when(c == 0)
            def _():
                acc[slot, :, out] = part

            @pl.when(c > 0)
            def _():
                acc[slot, :, out] += part

            return 0

        lax.fori_loop(0, depth // tile, piece, 0)

    def p_move(zz):
        return pltpu.make_async_remote_copy(
            src_ref=psend.at[zz],
            dst_ref=precv.at[zz],
            send_sem=p_send.at[zz],
            recv_sem=p_recv.at[zz],
            device_id=at(z, 1 - x, q),
            device_id_type=MESH,
        )

    def o_dst(zs, xx):
        return gin.at[
            pl.ds(pl.multiple_of(xx * half, half), half),
            pl.ds(pl.multiple_of(zs * depth, depth), depth),
        ]

    def o_move(zz, xt_, xs_, zs):
        return pltpu.make_async_remote_copy(
            src_ref=osend.at[zz],
            dst_ref=o_dst(zs, xs_),
            send_sem=o_send.at[zz, xt_],
            recv_sem=o_recv.at[zs, xs_],
            device_id=at(zz, xt_, q),
            device_id_type=MESH,
        )

    def exchange(slot, zz):
        theirs = pl.ds(pl.multiple_of((1 - x) * half, half), half)
        psend[zz] = acc[slot, theirs, :].astype(BF16)
        p_move(zz).start()

    def finish(slot, zz, own):
        ours = pl.ds(pl.multiple_of(x * half, half), half)
        p_move(zz).wait()
        osend[zz] = (acc[slot, ours, :] + precv[zz].astype(F32)).astype(BF16)
        if own:
            o_dst(z, x)[...] = osend[zz]
            o_move(zz, 1 - x, x, z).start()
        else:
            o_move(zz, x, x, z).start()
            o_move(zz, 1 - x, x, z).start()

    for j in range(nz):
        last = j == nz - 1
        if j == 1:
            own_x.start()
            for k in range(1, nz):
                x_move(lax.rem(z + k, nz), z).start()
        if last:
            own_x.wait()
            for k in range(1, nz):
                x_move(z, lax.rem(z + k, nz)).wait_recv()
            for k in range(xs.shape[0] // group):
                part = pl.ds(k * group, group)
                xt[:, part] = xs[part, :].T

        def step(c, _):
            if not last:
                for (_, zz, there), kind in zip(sources(j + 1), (UP, DOWN)):

                    def pass_on(zz=zz, kind=kind):
                        arrived(zz, q, c)
                        up_or_down(kind, zz, c)
                        send(ACROSS, zz, q, c)
                        send(TWIN, zz, q, c)

                    when(there, pass_on)
            for slot, zz, there in sources(j):

                def over(zz=zz):
                    arrived(zz, across, c)
                    send(TWIN, zz, across, c)

                when(there, over)

            if j > 0:
                @pl.when(c == 0)
                def _():
                    for slot, zz, there in sources(j - 1):
                        when(there, functools.partial(finish, slot, zz, j == 1))

            for slot, zz, there in sources(j):

                def use(slot=slot, zz=zz):
                    arrived(zz, twin, c)
                    arrived(zz, diagonal, c)
                    add_input(slot, zz, c)

                when(there, use)

            @pl.when(c == chunks - 1)
            def _():
                for slot, zz, there in sources(j):
                    when(there, functools.partial(exchange, slot, zz))

            if last:
                turn = lax.rem(c, 2)

                def out_copy(cc):
                    return pltpu.make_async_copy(
                        stage.at[turn], gw_out.at[:, columns(cc)], gw_sem.at[turn]
                    )

                @pl.when(c >= 2)
                def _():
                    out_copy(c - 2).wait()

                def piece(i, _):
                    here = pl.ds(pl.multiple_of(i * narrow, narrow), narrow)
                    there = pl.ds(pl.multiple_of(c * wide + i * narrow, narrow), narrow)
                    stage[turn, :, here] = jnp.dot(
                        xt[...], gh[:, there], preferred_element_type=F32
                    ).astype(BF16)
                    return 0

                lax.fori_loop(0, wide // narrow, piece, 0)
                out_copy(c).start()
            return 0

        lax.fori_loop(0, chunks, step, 0)

    for slot, zz, there in sources(nz - 1):
        when(there, functools.partial(finish, slot, zz, nz == 1))

    for k in range(nz):
        zs = lax.rem(z + k, nz)
        for xx in (x, 1 - x):
            if k == 0:
                continue
            o_move(zs, xx, xx, zs).wait_recv()
            o_move(zs, xx, x, z).wait_send()
    o_move(z, 1 - x, 1 - x, z).wait_recv()
    o_move(z, 1 - x, x, z).wait_send()
    gi_copy = pltpu.make_async_copy(gin, gi_out, gi_sem)
    gi_copy.start()
    for k in range(1, nz):
        x_move(lax.rem(z + k, nz), z).wait_send()
    everything = pl.ds(0, hidden)
    for zz in range(nz):
        for there, kind in (((z < nz - 1) & (z >= zz), UP), ((z > 0) & (z <= zz), DOWN)):
            pl.when(there)(
                lambda kind=kind, zz=zz: move(kind, zz, q, everything, 0).wait_send()
            )
        move(ACROSS, zz, q, everything, 0).wait_send()
        move(TWIN, zz, q, everything, 0).wait_send()
        move(TWIN, zz, across, everything, 0).wait_send()
    for c in range(max(chunks - 2, 0), chunks):
        pltpu.make_async_copy(
            stage.at[c % 2], gw_out.at[:, pl.ds(c * wide, wide)], gw_sem.at[c % 2]
        ).wait()
    gi_copy.wait()


def fused(nz, inputs, weight, grad_out, pre_act):
    group, model = inputs.shape
    depth, hidden = weight.shape
    rows = grad_out.shape[0]
    tokens = nz * group
    chunks = 12
    wide = hidden // chunks
    half = group // 2
    vmem = pl.BlockSpec(memory_space=pltpu.VMEM)
    hbm = pl.BlockSpec(memory_space=pl.ANY)
    dma = pltpu.SemaphoreType.DMA
    return pl.pallas_call(
        functools.partial(kernel, nz, chunks),
        out_shape=(
            jax.ShapeDtypeStruct((group, model), BF16),
            jax.ShapeDtypeStruct((depth, hidden), BF16),
        ),
        in_specs=[vmem, vmem, hbm, hbm],
        out_specs=(hbm, hbm),
        scratch_shapes=[
            pltpu.VMEM((tokens, hidden), BF16),
            pltpu.VMEM((depth, hidden), BF16),
            pltpu.VMEM((tokens, depth), BF16),
            pltpu.VMEM((depth, tokens), BF16),
            pltpu.VMEM((2, group, depth), F32),
            pltpu.VMEM((nz, half, depth), BF16),
            pltpu.VMEM((nz, half, depth), BF16),
            pltpu.VMEM((nz, half, depth), BF16),
            pltpu.VMEM((group, model), BF16),
            pltpu.VMEM((2, depth, wide), BF16),
            dma((4, nz, 4)),
            dma((nz, 4, chunks)),
            dma((nz,)),
            dma((nz,)),
            dma((nz,)),
            dma((nz,)),
            dma((nz, 2)),
            dma((nz, 2)),
            dma(()),
            dma((2,)),
            dma(()),
        ],
        compiler_params=pltpu.CompilerParams(
            collective_id=0, has_side_effects=True, vmem_limit_bytes=62 * 1024 * 1024
        ),
        cost_estimate=pl.CostEstimate(
            flops=4 * tokens * depth * hidden,
            bytes_accessed=4 * depth * hidden,
            transcendentals=rows * hidden,
        ),
    )(grad_out, pre_act, inputs, weight)


def plain(inputs, weight, grad_out, pre_act):
    grad_hidden = (grad_out.astype(F32) * gelu_slope(pre_act.astype(F32))).astype(BF16)
    input_cols = lax.all_to_all(inputs, "gx", split_axis=1, concat_axis=0, tiled=True)
    piece = lax.all_gather(grad_hidden, ("gx", "gz"), axis=0, tiled=True)
    weight_sum = lax.dot_general(
        input_cols, piece, (((0,), (0,)), ((), ())), preferred_element_type=F32
    )
    product = lax.dot_general(
        piece, weight, (((1,), (1,)), ((), ())), preferred_element_type=F32
    )
    summed = lax.psum(product, "gy").astype(BF16)
    grad_in = lax.all_to_all(summed, "gx", split_axis=0, concat_axis=1, tiled=True)
    return (grad_in, weight_sum.astype(BF16))


def solution(mesh):
    in_specs = (P("gx", "gz"), P(("gz", "gx"), "gy"), P(("gx", "gz"), "gy"), P(("gx", "gz"), "gy"))
    out_specs = (P("gx", "gz"), P(("gz", "gx"), "gy"))
    if mesh.shape["gy"] == 2 and mesh.shape["gz"] == 4 and mesh.shape["gx"] > 1:
        shards = functools.partial(fused, mesh.shape["gx"])
    else:
        shards = plain
    return jax.shard_map(shards, mesh=mesh, in_specs=in_specs, out_specs=out_specs, check_vma=False)
```

time: 340 us -> 241 us (0.71)
  Pallas kernels: 0 us -> 220 us
  blocking collectives: 137 us -> 0 us
  waiting for transfers between devices: 92.6 us -> 0 us
  matrix products: 51.4 us -> 0 us
  between operations: 14.1 us -> 0.64 us
  starting transfers between devices: 11.3 us -> 0 us
  local copies, waits for them, and re-layouts: 28.2 us -> 19.4 us
  other arithmetic: 4.56 us -> 0 us
    pallas_call x0 -> x1, Pallas kernels: none -> 220 us  [fused(): pl.pallas_call(functools.partial(kernel, nz, chunks), out_shape=(jax.Shap...]
    all_gather x1 -> x0, waiting for transfers between devices: 92.6 us -> none  [shards(): piece = lax.all_gather(grad_hidden, ('gx', 'gz'), axis=0, tiled=True)]
    psum x1 -> x0, blocking collectives: 77.5 us -> none  [shards(): summed = lax.psum(input_part, 'gy').astype(jnp.bfloat16)]
    all_to_all x1 -> x0, blocking collectives: 59.6 us -> none  [shards(): lax.all_to_all(inputs, 'gx', split_axis=1, concat_axis=0, tiled=True)]
    dot_general x2 -> x0, matrix products: 51.4 us -> none  [the longest x1 26.6 us: shards(): lax.dot_general(input_cols, piece, (((0,), (0,)), ((), ())), preferred_el...]
    all_to_all x1 -> x0, starting transfers between devices: 11.3 us -> none  [shards(): lax.all_to_all(summed, 'gx', split_axis=0, concat_axis=1, tiled=True)]
    unnamed x6 -> x2, local copies, waits for them, and re-layouts: 25.3 us -> 19.4 us
    convert_element_type x1 -> x0, other arithmetic: 4.56 us -> none  [shards(): (grad_out.astype(jnp.float32) * gelu_slope(pre_act.astype(jnp.float32)))....]
  transfers between devices with their start and end apart: 2 -> 0, of which waited for: 1 -> 0; matrix products, arithmetic and copies ran while one was open for 16% -> 0% of each run, Pallas kernels for 0% -> 0%
where the time goes in v1:
time: 241 us; the launch traced here: 240 us
  Pallas kernels  220 us (91%)
  local copies, waits for them, and re-layouts  19.4 us (8%)
    pallas_call x1, Pallas kernels, fused(): pl.pallas_call(functools.partial(kernel, nz, chunks), out_shape=(jax.Shap...  220 us
    unnamed x2, local copies, waits for them, and re-layouts  19.4 us

profile of v1, /device:TPU:0, one launch (start us, length us, event | category | flops | bytes accessed | tf_op | source)
XLA Modules:
  0.0 240.4 jit_solution(9650127847594489966)
XLA Ops:
  0.6 220.4 %shard_map.59 = (bf16[256,3072]{1,0:T(8,128)(2,1)}, bf16[768,12288]{1,0:T(8,128)(2,1)}) custom-call(bf16[64,12288]{1,0:T(8,128)(2,1)} %go.1, bf16[64,12288]{1,0:T(8,128)(2,1)} %pa.1, bf16[256,3072]{1,0:T(8,128)(2,1)} %x_hbm.1, bf16[768,12288]{1,0:T(8,128)(2,1)} %w_hbm.1), custom_call_target="tpu_custom_call" | custom-call | flops 38654705664 | bytes 37748736 | tf_op jit(solution)/shard_map/pallas_call | solution.py:326
  221.0 2.7 %copy.8 = bf16[256,3072]{1,0:T(8,128)(2,1)} copy(bf16[256,3072]{1,0:T(8,128)(2,1)} %get-tuple-element.4) | data formatting | bytes 3145728
  223.7 16.8 %copy.9 = bf16[768,12288]{1,0:T(8,128)(2,1)} copy(bf16[768,12288]{1,0:T(8,128)(2,1)} %get-tuple-element.5) | data formatting | bytes 37748736

commit v2 on v1

--- a/solution.py
+++ b/solution.py
@@ -108,26 +108,43 @@
     lax.fori_loop(0, chunks, make_own, 0)
     w_copy.wait()
 
+    def x_rows(zs, xx):
+        return xs.at[pl.ds(pl.multiple_of(zs * group + xx * half, half), half), :]
+
     def x_move(zt, zs):
         return pltpu.make_async_remote_copy(
-            src_ref=x_hbm.at[:, pl.ds(pl.multiple_of(zt * depth, depth), depth)],
-            dst_ref=xs.at[pl.ds(pl.multiple_of(zs * group, group), group), :],
-            send_sem=x_send.at[zt],
-            recv_sem=x_recv.at[zs],
+            src_ref=x_hbm.at[
+                pl.ds(pl.multiple_of(x * half, half), half),
+                pl.ds(pl.multiple_of(zt * depth, depth), depth),
+            ],
+            dst_ref=x_rows(zs, x),
+            send_sem=x_send.at[zt, 0],
+            recv_sem=x_recv.at[zs, x],
             device_id=at(zt, x, q),
+            device_id_type=MESH,
+        )
+
+    def x_share(zs, xx):
+        return pltpu.make_async_remote_copy(
+            src_ref=x_rows(zs, xx),
+            dst_ref=x_rows(zs, xx),
+            send_sem=x_send.at[zs, 1],
+            recv_sem=x_recv.at[zs, xx],
+            device_id=at(z, 1 - x, q),
             device_id_type=MESH,
         )
 
     own_x = pltpu.make_async_copy(
         x_hbm.at[:, pl.ds(pl.multiple_of(z * depth, depth), depth)],
         xs.at[pl.ds(pl.multiple_of(z * group, group), group), :],
-        x_recv.at[z],
+        x_recv.at[z, 0],
     )
 
     def sources(j):
         if j == 0:
             return [(0, z, None)]
-        return [(0, z - j, z >= j), (1, z + j, z + j < nz)]
+        first = 2 * (j % 2)
+        return [(first, z - j, z >= j), (first + 1, z + j, z + j < nz)]
 
     def when(condition, body):
         if condition is None:
@@ -175,15 +192,34 @@
             pl.ds(pl.multiple_of(zs * depth, depth), depth),
         ]
 
-    def o_move(zz, xt_, xs_, zs):
-        return pltpu.make_async_remote_copy(
-            src_ref=osend.at[zz],
-            dst_ref=o_dst(zs, xs_),
-            send_sem=o_send.at[zz, xt_],
-            recv_sem=o_recv.at[zs, xs_],
-            device_id=at(zz, xt_, q),
-            device_id_type=MESH,
-        )
+    def o_move(zt, zs):
+        return pltpu.make_async_remote_copy(
+            src_ref=osend.at[zt],
+            dst_ref=o_dst(zs, x),
+            send_sem=o_send.at[zt, 0],
+            recv_sem=o_recv.at[zs, x],
+            device_id=at(zt, x, q),
+            device_id_type=MESH,
+        )
+
+    def o_share(zs, xx):
+        return pltpu.make_async_remote_copy(
+            src_ref=o_dst(zs, xx),
+            dst_ref=o_dst(zs, xx),
+            send_sem=o_send.at[zs, 1],
+            recv_sem=o_recv.at[zs, xx],
+            device_id=at(z, 1 - x, q),
+            device_id_type=MESH,
+        )
+
+    def share_from(distance):
+        for zs, there in ((z - distance, z >= distance), (z + distance, z + distance < nz)):
+
+            def pass_over(zs=zs):
+                o_move(z, zs).wait_recv()
+                o_share(zs, x).start()
+
+            pl.when(there)(pass_over)
 
     def exchange(slot, zz):
         theirs = pl.ds(pl.multiple_of((1 - x) * half, half), half)
@@ -196,10 +232,9 @@
         osend[zz] = (acc[slot, ours, :] + precv[zz].astype(F32)).astype(BF16)
         if own:
             o_dst(z, x)[...] = osend[zz]
-            o_move(zz, 1 - x, x, z).start()
+            o_share(z, x).start()
         else:
-            o_move(zz, x, x, z).start()
-            o_move(zz, 1 - x, x, z).start()
+            o_move(zz, z).start()
 
     for j in range(nz):
         last = j == nz - 1
@@ -207,10 +242,14 @@
             own_x.start()
             for k in range(1, nz):
                 x_move(lax.rem(z + k, nz), z).start()
+        if j == max(nz - 2, 1):
+            for k in range(1, nz):
+                x_move(z, lax.rem(z + k, nz)).wait_recv()
+                x_share(lax.rem(z + k, nz), x).start()
         if last:
             own_x.wait()
             for k in range(1, nz):
-                x_move(z, lax.rem(z + k, nz)).wait_recv()
+                x_share(lax.rem(z + k, nz), 1 - x).wait_recv()
             for k in range(xs.shape[0] // group):
                 part = pl.ds(k * group, group)
                 xt[:, part] = xs[part, :].T
@@ -235,7 +274,7 @@
                 when(there, over)
 
             if j > 0:
-                @pl.when(c == 0)
+                @pl.when(c == 2)
                 def _():
                     for slot, zz, there in sources(j - 1):
                         when(there, functools.partial(finish, slot, zz, j == 1))
@@ -255,6 +294,11 @@
                     when(there, functools.partial(exchange, slot, zz))
 
             if last:
+                for distance in range(1, nz - 1):
+                    pl.when(c == chunks - 1 - 2 * (nz - 2 - distance))(
+                        functools.partial(share_from, distance)
+                    )
+
                 turn = lax.rem(c, 2)
 
                 def out_copy(cc):
@@ -283,19 +327,18 @@
     for slot, zz, there in sources(nz - 1):
         when(there, functools.partial(finish, slot, zz, nz == 1))
 
+    share_from(nz - 1)
     for k in range(nz):
         zs = lax.rem(z + k, nz)
-        for xx in (x, 1 - x):
-            if k == 0:
-                continue
-            o_move(zs, xx, xx, zs).wait_recv()
-            o_move(zs, xx, x, z).wait_send()
-    o_move(z, 1 - x, 1 - x, z).wait_recv()
-    o_move(z, 1 - x, x, z).wait_send()
+        o_share(zs, 1 - x).wait_recv()
+        o_share(zs, x).wait_send()
+        if k > 0:
+            o_move(zs, z).wait_send()
     gi_copy = pltpu.make_async_copy(gin, gi_out, gi_sem)
     gi_copy.start()
     for k in range(1, nz):
         x_move(lax.rem(z + k, nz), z).wait_send()
+        x_share(lax.rem(z + k, nz), x).wait_send()
     everything = pl.ds(0, hidden)
     for zz in range(nz):
         for there, kind in (((z < nz - 1) & (z >= zz), UP), ((z > 0) & (z <= zz), DOWN)):
@@ -336,7 +379,7 @@
             pltpu.VMEM((depth, hidden), BF16),
             pltpu.VMEM((tokens, depth), BF16),
             pltpu.VMEM((depth, tokens), BF16),
-            pltpu.VMEM((2, group, depth), F32),
+            pltpu.VMEM((4, group, depth), F32),
             pltpu.VMEM((nz, half, depth), BF16),
             pltpu.VMEM((nz, half, depth), BF16),
             pltpu.VMEM((nz, half, depth), BF16),
@@ -344,8 +387,8 @@
             pltpu.VMEM((2, depth, wide), BF16),
             dma((4, nz, 4)),
             dma((nz, 4, chunks)),
-            dma((nz,)),
-            dma((nz,)),
+            dma((nz, 2)),
+            dma((nz, 2)),
             dma((nz,)),
             dma((nz,)),
             dma((nz, 2)),

time: 241 us -> 219 us (0.909)
  Pallas kernels: 220 us -> 199 us
    pallas_call x1, Pallas kernels: 220 us -> 199 us  [fused(): pl.pallas_call(functools.partial(kernel, nz, chunks), out_shape=(jax.Shap...]
where the time goes in v2:
time: 219 us
  Pallas kernels  199 us (91%)
  local copies, waits for them, and re-layouts  19.4 us (9%)
    pallas_call x1, Pallas kernels, fused(): pl.pallas_call(functools.partial(kernel, nz, chunks), out_shape=(jax.Shap...  199 us
    unnamed x2, local copies, waits for them, and re-layouts  19.4 us

profile of v2, /device:TPU:0, one launch (start us, length us, event | category | flops | bytes accessed | tf_op | source)
XLA Modules:
  0.0 219.2 jit_solution(7773364481959951952)
XLA Ops:
  0.6 199.2 %shard_map.59 = (bf16[256,3072]{1,0:T(8,128)(2,1)}, bf16[768,12288]{1,0:T(8,128)(2,1)}) custom-call(bf16[64,12288]{1,0:T(8,128)(2,1)} %go.1, bf16[64,12288]{1,0:T(8,128)(2,1)} %pa.1, bf16[256,3072]{1,0:T(8,128)(2,1)} %x_hbm.1, bf16[768,12288]{1,0:T(8,128)(2,1)} %w_hbm.1), custom_call_target="tpu_custom_call" | custom-call | flops 38654705664 | bytes 37748736 | tf_op jit(solution)/shard_map/pallas_call | solution.py:369
  199.8 2.7 %copy.8 = bf16[256,3072]{1,0:T(8,128)(2,1)} copy(bf16[256,3072]{1,0:T(8,128)(2,1)} %get-tuple-element.4) | data formatting | bytes 3145728
  202.4 16.8 %copy.9 = bf16[768,12288]{1,0:T(8,128)(2,1)} copy(bf16[768,12288]{1,0:T(8,128)(2,1)} %get-tuple-element.5) | data formatting | bytes 37748736

commit v3 on v2

--- a/solution.py
+++ b/solution.py
@@ -23,9 +23,9 @@
 def kernel(
     nz, chunks,
     go, pa, x_hbm, w_hbm,
-    gi_out, gw_out,
+    gi_out, gw_out, far_out,
     gh, w, xs, xt, acc, psend, precv, osend, gin, stage,
-    ring_send, ring_recv, x_send, x_recv, p_send, p_recv, o_send, o_recv, w_sem, gw_sem, gi_sem,
+    ring_send, ring_recv, x_send, x_recv, p_send, p_recv, o_send, o_recv, w_sem, gw_sem, gi_sem, far_sem,
 ):
     z, x, q = lax.axis_index("gx"), lax.axis_index("gy"), lax.axis_index("gz")
     rows = go.shape[0]
@@ -226,11 +226,15 @@
         psend[zz] = acc[slot, theirs, :].astype(BF16)
         p_move(zz).start()
 
-    def finish(slot, zz, own):
+    def finish(slot, zz, own, far):
         ours = pl.ds(pl.multiple_of(x * half, half), half)
         p_move(zz).wait()
         osend[zz] = (acc[slot, ours, :] + precv[zz].astype(F32)).astype(BF16)
-        if own:
+        if far:
+            for xx in range(2):
+                o_dst(zz, xx)[...] = jnp.zeros((half, depth), BF16)
+            pltpu.make_async_copy(osend.at[zz], far_out, far_sem).start()
+        elif own:
             o_dst(z, x)[...] = osend[zz]
             o_share(z, x).start()
         else:
@@ -277,7 +281,7 @@
                 @pl.when(c == 2)
                 def _():
                     for slot, zz, there in sources(j - 1):
-                        when(there, functools.partial(finish, slot, zz, j == 1))
+                        when(there, functools.partial(finish, slot, zz, j == 1, False))
 
             for slot, zz, there in sources(j):
 
@@ -325,15 +329,18 @@
         lax.fori_loop(0, chunks, step, 0)
 
     for slot, zz, there in sources(nz - 1):
-        when(there, functools.partial(finish, slot, zz, nz == 1))
-
-    share_from(nz - 1)
+        when(there, functools.partial(finish, slot, zz, False, True))
+
     for k in range(nz):
         zs = lax.rem(z + k, nz)
-        o_share(zs, 1 - x).wait_recv()
-        o_share(zs, x).wait_send()
-        if k > 0:
-            o_move(zs, z).wait_send()
+
+        def settle(zs=zs, k=k):
+            o_share(zs, 1 - x).wait_recv()
+            o_share(zs, x).wait_send()
+            if k > 0:
+                o_move(zs, z).wait_send()
+
+        pl.when((zs - z < nz - 1) & (z - zs < nz - 1))(settle)
     gi_copy = pltpu.make_async_copy(gin, gi_out, gi_sem)
     gi_copy.start()
     for k in range(1, nz):
@@ -353,6 +360,29 @@
             stage.at[c % 2], gw_out.at[:, pl.ds(c * wide, wide)], gw_sem.at[c % 2]
         ).wait()
     gi_copy.wait()
+    for _, zz, there in sources(nz - 1):
+        when(there, lambda zz=zz: pltpu.make_async_copy(osend.at[zz], far_out, far_sem).wait())
+
+
+def hand_on(source, target):
+    target[...] = source[...]
+
+
+def handed_on(array):
+    size, columns = array.shape
+    part = 64 if size % 64 == 0 else size
+    block = pl.BlockSpec((part, columns), lambda i: (i, 0))
+    return pl.pallas_call(
+        hand_on,
+        grid=(size // part,),
+        out_shape=jax.ShapeDtypeStruct(array.shape, array.dtype),
+        in_specs=[block],
+        out_specs=block,
+        compiler_params=pltpu.CompilerParams(vmem_limit_bytes=60 * 1024 * 1024),
+        cost_estimate=pl.CostEstimate(
+            flops=0, bytes_accessed=4 * size * columns, transcendentals=0
+        ),
+    )(array)
 
 
 def fused(nz, inputs, weight, grad_out, pre_act):
@@ -366,14 +396,15 @@
     vmem = pl.BlockSpec(memory_space=pltpu.VMEM)
     hbm = pl.BlockSpec(memory_space=pl.ANY)
     dma = pltpu.SemaphoreType.DMA
-    return pl.pallas_call(
+    grad_in, grad_weight, far = pl.pallas_call(
         functools.partial(kernel, nz, chunks),
         out_shape=(
             jax.ShapeDtypeStruct((group, model), BF16),
             jax.ShapeDtypeStruct((depth, hidden), BF16),
+            jax.ShapeDtypeStruct((half, depth), BF16),
         ),
         in_specs=[vmem, vmem, hbm, hbm],
-        out_specs=(hbm, hbm),
+        out_specs=(hbm, hbm, hbm),
         scratch_shapes=[
             pltpu.VMEM((tokens, hidden), BF16),
             pltpu.VMEM((depth, hidden), BF16),
@@ -396,6 +427,7 @@
             dma(()),
             dma((2,)),
             dma(()),
+            dma(()),
         ],
         compiler_params=pltpu.CompilerParams(
             collective_id=0, has_side_effects=True, vmem_limit_bytes=62 * 1024 * 1024
@@ -406,6 +438,19 @@
             transcendentals=rows * hidden,
         ),
     )(grad_out, pre_act, inputs, weight)
+    z, x = lax.axis_index("gx"), lax.axis_index("gy")
+    end = 2 * (nz - 1)
+    ours = lax.ppermute(far, "gx", [(0, nz - 1), (nz - 1, 0)])
+    theirs = lax.ppermute(
+        far, ("gx", "gy"), [(0, end + 1), (1, end), (end, 1), (end + 1, 0)]
+    )
+    grad_weight = handed_on(grad_weight)
+    pair = jnp.where(
+        x == 0, jnp.concatenate([ours, theirs]), jnp.concatenate([theirs, ours])
+    )
+    place = lax.broadcasted_iota(jnp.int32, (1, model), 1) // depth
+    spread = jnp.where(jnp.abs(place - z) == nz - 1, jnp.concatenate([pair] * nz, axis=1), grad_in)
+    return spread, grad_weight
 
 
 def plain(inputs, weight, grad_out, pre_act):

time: 219 us -> 221 us (level)
  local copies, waits for them, and re-layouts: 19.4 us -> 0.01 us
  Pallas kernels: 199 us -> 210 us
  starting transfers between devices: 0 us -> 9.1 us
    unnamed x2, local copies, waits for them, and re-layouts: 19.4 us -> 0.01 us
    pallas_call x0 -> x1, Pallas kernels: none -> 16.9 us  [handed_on(): pl.pallas_call(hand_on, grid=(size // part,), out_shape=jax.ShapeDtypeStr...]
    ppermute x0 -> x2, starting transfers between devices: none -> 9.1 us  [the longest x1 5.08 us: fused(): ours = lax.ppermute(far, 'gx', [(0, nz - 1), (nz - 1, 0)])]
    pallas_call x1, Pallas kernels: 199 us -> 193 us  [fused(): pl.pallas_call(functools.partial(kernel, nz, chunks), out_shape=(jax.Shap...]
  transfers between devices with their start and end apart: 0 -> 2, of which waited for: 0 -> 0; matrix products, arithmetic and copies ran while one was open for 0% -> 0% of each run, Pallas kernels for 0% -> 8%
where the time goes in v3:
time: 221 us
  Pallas kernels  210 us (95%)
  starting transfers between devices  9.1 us (4%)
    pallas_call x1, Pallas kernels, fused(): pl.pallas_call(functools.partial(kernel, nz, chunks), out_shape=(jax.Shap...  193 us
    pallas_call x1, Pallas kernels, handed_on(): pl.pallas_call(hand_on, grid=(size // part,), out_shape=jax.ShapeDtypeStr...  16.9 us
    ppermute x1, starting transfers between devices, fused(): ours = lax.ppermute(far, 'gx', [(0, nz - 1), (nz - 1, 0)])  5.08 us
  transfers between devices with their start and end apart: 2, of which 0 were waited for; matrix products, arithmetic and copies ran while one was open for 0% of the time, Pallas kernels for 8%

profile of v3, /device:TPU:0, one launch (start us, length us, event | category | flops | bytes accessed | tf_op | source)
XLA Modules:
  0.0 221.0 jit_solution(15170325635524951801)
XLA Ops:
  0.6 192.6 %shard_map.59 = (bf16[256,3072]{1,0:T(8,128)(2,1)}, bf16[768,12288]{1,0:T(8,128)(2,1)}, bf16[128,768]{1,0:T(8,128)(2,1)}) custom-call(bf16[64,12288]{1,0:T(8,128)(2,1)} %go.1, bf16[64,12288]{1,0:T(8,128)(2,1)} %pa.1, bf16[256,3072]{1,0:T(8,128)(2,1)} %x_hbm.1, bf16[768,12288]{1,0:T(8,128)(2,1)} %w_hbm.1), custom_call_target="tpu_custom_call" | custom-call | flops 38654705664 | bytes 37748736 | tf_op jit(solution)/shard_map/pallas_call | solution.py:399
  193.2 4.0 %collective-permute-start.1 = (bf16[128,768]{1,0:T(8,128)(2,1)}, bf16[128,768]{1,0:T(8,128)(2,1)S(1)}, u32[]{:S(2)}, u32[]{:S(2)}) collective-permute-start(bf16[128,768]{1,0:T(8,128)(2,1)} %get-tuple-element.5), channel_id=1, source_target_pairs={{0,28},{4,24},{24,4},{28,0},{1,29},{5,25},{25,5},{29,1},{2,30},{6,... | collective-permute-start | bytes 589832 | tf_op jit(solution)/shard_map/ppermute | solution.py:444
  197.2 5.1 %collective-permute-start = (bf16[128,768]{1,0:T(8,128)(2,1)}, bf16[128,768]{1,0:T(8,128)(2,1)S(1)}, u32[]{:S(2)}, u32[]{:S(2)}) collective-permute-start(bf16[128,768]{1,0:T(8,128)(2,1)} %get-tuple-element.5), channel_id=1, source_target_pairs={{0,24},{24,0},{1,25},{25,1},{2,26},{26,2},{3,27},{27,3},{4,28},{28... | collective-permute-start | bytes 589832 | tf_op jit(solution)/shard_map/ppermute | solution.py:443
  202.3 0.0 copy-start
  202.3 16.9 %shard_map.60 = bf16[768,12288]{1,0:T(8,128)(2,1)} custom-call(bf16[768,12288]{1,0:T(8,128)(2,1)} %get-tuple-element.7.source), custom_call_target="tpu_custom_call" | custom-call | bytes 37748736 | tf_op jit(solution)/shard_map/pallas_call | solution.py:375
  219.3 0.0 collective-permute-done.1
  219.3 0.0 collective-permute-done
  219.3 0.1 maximum_select_fusion.1
  219.4 0.0 copy-done
  219.4 1.6 maximum_select_fusion
  (1 shorter events, 0.0 us)
Async XLA Ops:
  193.2 26.1 %collective-permute-start.1 = (bf16[128,768]{1,0:T(8,128)(2,1)}, bf16[128,768]{1,0:T(8,128)(2,1)S(1)}, u32[]{:S(2)}, u32[]{:S(2)}) collective-permute-start(bf16[128,768]{1,0:T(8,128)(2,1)} %get-tuple-element.5), channel_id=1, source_target_pairs={{0,28},{4,24},{24,4},{28,0},{1,29},{5,25},{25,5},{29,1},{2,30},{6,... | collective-permute-start | bytes 589832 | tf_op jit(solution)/shard_map/ppermute | solution.py:444
  197.2 22.1 %collective-permute-start = (bf16[128,768]{1,0:T(8,128)(2,1)}, bf16[128,768]{1,0:T(8,128)(2,1)S(1)}, u32[]{:S(2)}, u32[]{:S(2)}) collective-permute-start(bf16[128,768]{1,0:T(8,128)(2,1)} %get-tuple-element.5), channel_id=1, source_target_pairs={{0,24},{24,0},{1,25},{25,1},{2,26},{26,2},{3,27},{27,3},{4,28},{28... | collective-permute-start | bytes 589832 | tf_op jit(solution)/shard_map/ppermute | solution.py:443
  202.3 17.1 %copy-start = (bf16[256,3072]{1,0:T(8,128)(2,1)S(1)}, bf16[256,3072]{1,0:T(8,128)(2,1)}, u32[]{:S(2)}) copy-start(bf16[256,3072]{1,0:T(8,128)(2,1)} %get-tuple-element.6) | copy-start | bytes 4718596

commit v4 on v2

--- a/solution.py
+++ b/solution.py
@@ -360,7 +360,7 @@
     depth, hidden = weight.shape
     rows = grad_out.shape[0]
     tokens = nz * group
-    chunks = 12
+    chunks = 16
     wide = hidden // chunks
     half = group // 2
     vmem = pl.BlockSpec(memory_space=pltpu.VMEM)

time: 219 us -> 231 us (1.055)
  Pallas kernels: 199 us -> 211 us
    pallas_call x1, Pallas kernels: 199 us -> 211 us  [fused(): pl.pallas_call(functools.partial(kernel, nz, chunks), out_shape=(jax.Shap...]
where the time goes in v4:
time: 231 us
  Pallas kernels  211 us (91%)
  local copies, waits for them, and re-layouts  19.4 us (8%)
    pallas_call x1, Pallas kernels, fused(): pl.pallas_call(functools.partial(kernel, nz, chunks), out_shape=(jax.Shap...  211 us
    unnamed x2, local copies, waits for them, and re-layouts  19.4 us

profile of v4, /device:TPU:0, one launch (start us, length us, event | category | flops | bytes accessed | tf_op | source)
XLA Modules:
  0.0 231.0 jit_solution(8906604454370551284)
XLA Ops:
  0.6 210.9 %shard_map.59 = (bf16[256,3072]{1,0:T(8,128)(2,1)}, bf16[768,12288]{1,0:T(8,128)(2,1)}) custom-call(bf16[64,12288]{1,0:T(8,128)(2,1)} %go.1, bf16[64,12288]{1,0:T(8,128)(2,1)} %pa.1, bf16[256,3072]{1,0:T(8,128)(2,1)} %x_hbm.1, bf16[768,12288]{1,0:T(8,128)(2,1)} %w_hbm.1), custom_call_target="tpu_custom_call" | custom-call | flops 38654705664 | bytes 37748736 | tf_op jit(solution)/shard_map/pallas_call | solution.py:369
  211.6 2.7 %copy.8 = bf16[256,3072]{1,0:T(8,128)(2,1)} copy(bf16[256,3072]{1,0:T(8,128)(2,1)} %get-tuple-element.4) | data formatting | bytes 3145728
  214.2 16.8 %copy.9 = bf16[768,12288]{1,0:T(8,128)(2,1)} copy(bf16[768,12288]{1,0:T(8,128)(2,1)} %get-tuple-element.5) | data formatting | bytes 37748736
